TPU v7x, 32 devices: a whole 2x2x4 slice. The times are simulated.
32 devices in a mesh: gz: 4 (over y, x), xy: 8 (over z, core).
Axes of the slice: x: 2, y: 2, z: 4, core: 2. Of those that a mesh axis runs over, the one named last changes fastest.
Arguments:
- populations: float32 [19, 128, 32, 128], P(None, 'gz', 'xy'), as said below
- field_gain: float32 [128], P('gz'), may hold values from 0.05 to 0.4
- front_depth: int32 [8, 32], P('xy'), may hold values from 0 to 31, as said below
- phase: float32 [32, 256, 1024], P(None, 'xy', 'gz'), may hold values from 0 to 1
- solute: float32 [32, 256, 1024], P(None, 'xy', 'gz'), may hold values from 0.5 to 1.5
Outputs:
- velocity: float32 [3, 128, 32, 128], P(None, 'gz', 'xy')
- phase_next: float32 [32, 256, 1024], P(None, 'xy', 'gz')
- solute_next: float32 [32, 256, 1024], P(None, 'xy', 'gz')
Inputs may be any that keep to these rules, and one draw needn't show every extreme that they name: Every cell's populations are positive and within a fifth of a lattice equilibrium of density near 1 and speed below 0.2. `front_depth`: depth indices of the front tiles, from 0 to 31.
All inputs are finite; a program needn't handle non-finite values.
Results may differ from a plain program's by a relative error of at most 0.0003.
Values sent between devices are 32-bit elements; how exact they have to be, the bound alone decides.
A program may use at most 128 MiB of HBM per device.

v0:
```python
import functools
import math

import jax
import jax.numpy as jnp
import numpy as np
from jax import lax
from jax.experimental import pallas as pl
from jax.experimental.pallas import tpu as pltpu
from jax.sharding import PartitionSpec as P

MESH = pl.DeviceIdType.MESH
F32 = jnp.float32

PAIRS = (
    (1, 2, (1, 0, 0), 1.0 / 18.0),
    (3, 4, (0, 1, 0), 1.0 / 18.0),
    (5, 6, (0, 0, 1), 1.0 / 18.0),
    (7, 8, (1, 1, 0), 1.0 / 36.0),
    (9, 10, (1, -1, 0), 1.0 / 36.0),
    (11, 12, (1, 0, 1), 1.0 / 36.0),
    (13, 14, (1, 0, -1), 1.0 / 36.0),
    (15, 16, (0, 1, 1), 1.0 / 36.0),
    (17, 18, (0, 1, -1), 1.0 / 36.0),
)


def weights_of(fine):
    numer = 2 * fine + 9
    return numer // 16, (numer % 16) / 16.0


def col_table():
    table = np.zeros((128, 512), np.float32)
    for par in range(2):
        for fine in range(256):
            tile, inner = fine // 32, fine % 32
            low, frac = weights_of(inner)
            for off, weight in ((low, 1.0 - frac), (low + 1, frac)):
                if off == 0:
                    rim, j = 1, 0
                elif off == 5:
                    rim, j = 1, 3
                else:
                    rim, j = 0, off - 1
                table[par * 64 + rim * 32 + tile * 4 + j, par * 256 + fine] += weight
    return table


def row_table():
    table = np.zeros((32, 8), np.float32)
    for fine in range(32):
        low, frac = weights_of(fine)
        for off, weight in ((low, 1.0 - frac), (low + 1, frac)):
            place = 4 if off == 0 else off if off == 5 else off - 1
            table[fine, place] += 0.2 * weight
    return table


def force_table(lanes, width_y):
    width_x = 4 * lanes
    x = (np.arange(width_x) + 0.5) * (2.0 * math.pi / width_x)
    y = (np.arange(width_y) + 0.5) * (2.0 * math.pi / width_y)
    ax = np.tile(x.reshape(lanes, 4), (1, 2))[:, :, None]
    ay = y[None, None, :]
    full = (lanes, 8, width_y)
    return np.stack(
        [
            np.broadcast_to(np.cos(ax - 0.7), full),
            np.broadcast_to(np.sin(ay + 0.7), full),
            np.cos(ax + ay),
        ],
        axis=1,
    ).astype(np.float32)


def kernel(
    slabs, lanes,
    pop, gain, depth, phase, solute, ftab, ctab, rtab,
    vel, p_out, s_out,
    sums, xs, xr, zr, dr, vs, vr, v8, v8r, pk, wr, fine, ex, hx, ey, hy, p1, s1,
    send, recv,
):
    gz, xy = lax.axis_index("gz"), lax.axis_index("xy")

    def at(dz, dx):
        return (lax.rem(gz + dz + slabs, slabs), lax.rem(xy + dx + lanes, lanes))

    peers = [(1, 0), (-1, 0), (0, 1), (0, -1), (1, 1), (1, -1), (-1, 1), (-1, -1)]
    peers += [(d, 0) for d in range(2, slabs - 1)]
    barrier = pltpu.get_barrier_semaphore()
    for peer in peers:
        pl.semaphore_signal(barrier, inc=1, device_id=at(*peer), device_id_type=MESH)

    count = [0]

    def remote(src, dst, where):
        i = count[0]
        count[0] += 1
        copy = pltpu.make_async_remote_copy(
            src_ref=src, dst_ref=dst, send_sem=send.at[i], recv_sem=recv.at[i],
            device_id=at(*where), device_id_type=MESH,
        )
        copy.start()
        return copy

    rows32 = lax.broadcasted_iota(jnp.int32, (128, 32), 0) // 4
    cols32 = lax.broadcasted_iota(jnp.int32, (128, 32), 1)
    gain_col = jnp.sum(jnp.where(rows32 == cols32, gain[...], 0.0), axis=1, keepdims=True)
    shape = ftab[xy]
    force = [
        jnp.broadcast_to(shape[c][None], (16, 8, 128)).reshape(128, 128) * gain_col
        for c in range(3)
    ]
    for c in range(3):
        vel[c] = force[c]

    def collide(i, carry):
        at_rows = pl.ds(pl.multiple_of(i * 8, 8), 8)
        f = [pop[q, at_rows, :] for q in range(19)]
        fc = [vel[c, at_rows, :] for c in range(3)]
        rho = f[0]
        mom = [0.5 * fc[0], 0.5 * fc[1], 0.5 * fc[2]]
        for a, b, e, _ in PAIRS:
            rho = rho + (f[a] + f[b])
            odd = f[a] - f[b]
            for c in range(3):
                if e[c] > 0:
                    mom[c] = mom[c] + odd
                elif e[c] < 0:
                    mom[c] = mom[c] - odd
        inv = 1.0 / rho
        u = [m * inv for m in mom]
        speed = u[0] * u[0] + u[1] * u[1] + u[2] * u[2]
        work = u[0] * fc[0] + u[1] * fc[1] + u[2] * fc[2]
        base = 1.25 * rho * (1.0 - 1.5 * speed) - 1.125 * work
        rho_a = 5.625 * rho
        rho_b = 3.75 * rho
        post = [None] * 19
        post[0] = -0.25 * f[0] + (1.0 / 3.0) * base

        def along(v, e):
            total = None
            for c in range(3):
                if e[c]:
                    term = v[c] if e[c] > 0 else -v[c]
                    total = term if total is None else total + term
            return total

        for a, b, e, w in PAIRS:
            cu, cf = along(u, e), along(fc, e)
            even = w * (base + cu * (rho_a * cu + 3.375 * cf))
            odd = w * (rho_b * cu + 1.125 * cf)
            post[a] = -0.25 * f[a] + (even + odd)
            post[b] = -0.25 * f[b] + (even - odd)

        def up(q):
            return pltpu.roll(post[q], 1, 1)

        def down(q):
            return pltpu.roll(post[q], 127, 1)

        def put(n, middle, plus, minus):
            a, b = up(plus), down(minus)
            sums[n, at_rows, :] = post[middle] + (a + b)
            sums[n + 1, at_rows, :] = a - b

        put(0, 1, 11, 13)
        sums[2, at_rows, :] = post[7]
        sums[3, at_rows, :] = post[9]
        put(4, 2, 14, 12)
        sums[6, at_rows, :] = post[10]
        sums[7, at_rows, :] = post[8]
        put(8, 3, 15, 17)
        put(10, 4, 18, 16)
        put(12, 0, 5, 6)
        return carry

    lax.fori_loop(0, 16, collide, 0)

    row = lax.broadcasted_iota(jnp.int32, (128, 128), 0)
    x_of = lax.rem(row, 4)
    plus_ids, minus_ids = (8, 9, 2, 6), (10, 11, 3, 7)

    def roll0(v, s):
        s = s % v.shape[0]
        return v if s == 0 else pltpu.roll(v, s, 0)

    def merge(values):
        out = values[-1]
        for m in range(len(values) - 1):
            out = jnp.where(x_of == m, values[m], out)
        return out

    xs[0] = merge([roll0(sums[i], m - 3) for m, i in enumerate(plus_ids)])
    xs[1] = merge([roll0(sums[i], m) for m, i in enumerate(minus_ids)])

    pl.semaphore_wait(barrier, len(peers))
    flow_copies = [
        remote(xs.at[0], xr.at[0], (0, 1)),
        remote(xs.at[1], xr.at[1], (0, -1)),
        remote(sums.at[pl.ds(0, 4), pl.ds(120, 8)], zr.at[0], (1, 0)),
        remote(sums.at[pl.ds(4, 4), pl.ds(0, 8)], zr.at[1], (-1, 0)),
        remote(sums.at[2, pl.ds(120, 8)], dr.at[0], (1, 1)),
        remote(sums.at[3, pl.ds(120, 8)], dr.at[1], (1, -1)),
        remote(sums.at[6, pl.ds(0, 8)], dr.at[2], (-1, 1)),
        remote(sums.at[7, pl.ds(0, 8)], dr.at[3], (-1, -1)),
    ]

    lane = lax.broadcasted_iota(jnp.int32, (32, 128), 1)

    def edges(k, carry):
        first, last = carry
        for n, ref in enumerate((phase, solute)):
            ex[0, 0, n, pl.ds(k, 1), :] = ref[k, 31:32, :]
            ex[0, 1, n, pl.ds(k, 1), :] = ref[k, 0:1, :]
            here = lane == k + 32 * n
            last = jnp.where(here, ref[k, :, 255:256], last)
            first = jnp.where(here, ref[k, :, 0:1], first)
        return first, last

    nothing = jnp.zeros((32, 128), F32)
    first, last = lax.fori_loop(0, 32, edges, (nothing, nothing))
    ey[0, 0] = last
    ey[0, 1] = first

    def send_edges(turn):
        return [
            remote(ex.at[turn, 0], hx.at[turn, 0], (0, 1)),
            remote(ex.at[turn, 1], hx.at[turn, 1], (0, -1)),
            remote(ey.at[turn, 0], hy.at[turn, 0], (1, 0)),
            remote(ey.at[turn, 1], hy.at[turn, 1], (-1, 0)),
        ]

    band_copies = send_edges(0)
    for copy in flow_copies:
        copy.wait()

    sub = lax.broadcasted_iota(jnp.int32, (8, 128), 0)

    def shift_x(i, sign):
        if sign > 0:
            m = plus_ids.index(i)
            return jnp.where(x_of == 0, roll0(xr[0], -m), roll0(sums[i], 1))
        m = minus_ids.index(i)
        return jnp.where(x_of == 3, roll0(xr[1], 3 - m), roll0(sums[i], -1))

    def shift_z(value, sign, block):
        moved = roll0(value, 4 * sign)
        if sign > 0:
            return jnp.concatenate([jnp.where(sub < 4, block, moved[:8]), moved[8:]], axis=0)
        return jnp.concatenate([moved[:120], jnp.where(sub >= 4, block, moved[120:])], axis=0)

    rho = sums[12]
    my = sums[13]
    a = shift_x(8, 1)
    b = shift_x(10, -1)
    rho = rho + (a + b)
    mx = a - b
    my = my + (shift_x(9, 1) + shift_x(11, -1))
    a = shift_z(sums[0], 1, roll0(zr[0, 0], 4))
    b = shift_z(sums[4], -1, roll0(zr[1, 0], 4))
    rho = rho + (a + b)
    mz = a - b
    my = my + shift_z(sums[1], 1, roll0(zr[0, 1], 4))
    my = my + shift_z(sums[5], -1, roll0(zr[1, 1], 4))
    a = shift_z(shift_x(2, 1), 1, jnp.where(sub == 0, roll0(dr[0], 1), roll0(zr[0, 2], 5)))
    b = shift_z(shift_x(7, -1), -1, jnp.where(sub == 7, roll0(dr[3], 7), roll0(zr[1, 3], 3)))
    rho = rho + (a + b)
    mz = mz + (a - b)
    mx = mx + (a - b)
    a = shift_z(shift_x(3, -1), 1, jnp.where(sub == 3, roll0(dr[1], 7), roll0(zr[0, 3], 3)))
    b = shift_z(shift_x(6, 1), -1, jnp.where(sub == 4, roll0(dr[2], 1), roll0(zr[1, 2], 5)))
    rho = rho + (a + b)
    mz = mz + (a - b)
    mx = mx - (a - b)
    inv = 1.0 / rho
    v = [(m + 0.5 * vel[c]) * inv for c, m in enumerate((mz, mx, my))]
    for c in range(3):
        vel[c] = v[c]
    vs[0] = merge([roll0(v[c], c - 3) for c in range(3)])
    vs[1] = merge([roll0(v[c], c) for c in range(3)])
    rim_copies = [
        remote(vs.at[0], vr.at[0], (0, 1)),
        remote(vs.at[1], vr.at[1], (0, -1)),
    ]
    for copy in rim_copies:
        copy.wait()

    sub128 = lax.rem(row, 8)
    lane128 = lax.broadcasted_iota(jnp.int32, (128, 128), 1)
    lane_in = lax.rem(lane128, 4)
    for c in range(3):
        own = vel[c]
        for par in range(2):
            block = jnp.where(
                sub128 == 4,
                roll0(vr[0], 4 - c - 4 * par),
                jnp.where(sub128 == 5, roll0(vr[1], 5 - c - 4 * par), roll0(own, -4 * par)),
            )
            v8[c, par] = block.reshape(16, 8, 128)
            side = jnp.where(lane_in == 0, pltpu.roll(block, 1, 1), pltpu.roll(block, 127, 1))
            v8r[c, par] = side.reshape(16, 8, 128)

    lane8 = lax.broadcasted_iota(jnp.int32, (8, 128), 1)
    tile_of = lane8 // 4
    group_of = lane8 // 32
    total_z = 32 * slabs
    none8 = jnp.zeros((8, 128), F32)
    for c in range(3):

        def gather(tile, carry):
            carry = list(carry)
            start = depth[0, tile] * 4 - 1 + total_z
            for dz in range(6):
                z = lax.rem(start + dz, total_z)
                z_here = lax.rem(z, 32)
                mark = jnp.where(z // 32 == gz, tile, -1)
                here = tile_of == mark
                par, half = lax.rem(z_here, 2), z_here // 2
                carry[2 * dz] = jnp.where(here, v8[c, par, half], carry[2 * dz])
                carry[2 * dz + 1] = jnp.where(here, v8r[c, par, half], carry[2 * dz + 1])
            return tuple(carry)

        items = lax.fori_loop(0, 8 * slabs, gather, (none8,) * 12)
        for target in range(slabs):
            for m in range(3):
                out = none8
                for g in range(4):
                    item = items[4 * m + g]
                    s = (32 * (g - target)) % 128
                    moved = item if s == 0 else pltpu.roll(item, s, 1)
                    out = jnp.where(group_of == g, moved, out)
                pk[target, 3 * c + m] = out

    window_copies = [
        remote(pk.at[lax.rem(gz + d, slabs)], wr.at[d - 1], (d, 0)) for d in range(1, slabs)
    ]
    windows = pk[gz]
    for d, copy in enumerate(window_copies):
        copy.wait()
        windows = windows + wr[d]
    wide = jnp.dot(
        windows.reshape(72, 128), ctab[...],
        precision=lax.Precision.HIGHEST, preferred_element_type=F32,
    )
    for c in range(3):
        for dz in range(6):
            at_row = (3 * c + dz // 2) * 8
            at_col = (dz % 2) * 256
            fine[c, dz] = jnp.dot(
                rtab[...], wide[at_row:at_row + 8, at_col:at_col + 256],
                precision=lax.Precision.HIGHEST, preferred_element_type=F32,
            )

    big_row = lax.broadcasted_iota(jnp.int32, (32, 256), 0)
    big_lane = lax.broadcasted_iota(jnp.int32, (32, 256), 1)

    def band(turn, src, dst):
        def plane(k, carry):
            before, after, first, last = carry
            low = (2 * k + 9) // 16
            frac = lax.rem(2 * k + 9, 16).astype(F32) * (1.0 / 16.0)
            flow = []
            for c in range(3):
                lower = fine[c, low]
                flow.append(lower + frac * (fine[c, low + 1] - lower))
            above, below = jnp.minimum(k + 1, 31), jnp.maximum(k - 1, 0)
            results = []
            for n, ref in enumerate(src):
                mid = ref[k]
                zu, zd = ref[above], ref[below]
                xu = jnp.where(
                    big_row == 31, hx[turn, 1, n, pl.ds(k, 1), :], pltpu.roll(mid, 31, 0)
                )
                xd = jnp.where(
                    big_row == 0, hx[turn, 0, n, pl.ds(k, 1), :], pltpu.roll(mid, 1, 0)
                )
                yu = jnp.where(
                    big_lane == 255, after[:, 32 * n:32 * n + 1], pltpu.roll(mid, 255, 1)
                )
                yd = jnp.where(
                    big_lane == 0, before[:, 32 * n:32 * n + 1], pltpu.roll(mid, 1, 1)
                )
                drift = flow[0] * (zu - zd) + flow[1] * (xu - xd) + flow[2] * (yu - yd)
                zz = zu + zd
                side = (xu + xd) + (yu + yd)
                results.append((mid, zz, side, drift))
            p, zz, side, drift = results[0]
            s = results[1][0]
            drive = p * (1.0 - p) * (0.4 * p + 0.2 * s - 0.4)
            change = 0.15 * zz + 0.1 * side - 0.7 * p - drift + drive
            p_new = p + change
            s, zz, side, drift = results[1]
            s_new = 0.4 * s + 0.1 * (zz + side) - drift + 0.85 * s * change
            dst[0][k] = p_new
            dst[1][k] = s_new
            if turn == 0:
                for n, new in enumerate((p_new, s_new)):
                    ex[1, 0, n, pl.ds(k, 1), :] = new[31:32, :]
                    ex[1, 1, n, pl.ds(k, 1), :] = new[0:1, :]
                    here = lane == k + 32 * n
                    last = jnp.where(here, new[:, 255:256], last)
                    first = jnp.where(here, new[:, 0:1], first)
            return pltpu.roll(before, 127, 1), pltpu.roll(after, 127, 1), first, last

        return lax.fori_loop(0, 32, plane, (hy[turn, 0], hy[turn, 1], nothing, nothing))

    for copy in band_copies:
        copy.wait()
    _, _, first, last = band(0, (phase, solute), (p1, s1))
    ey[1, 0] = last
    ey[1, 1] = first
    for copy in send_edges(1):
        copy.wait()
    band(1, (p1, s1), (p_out, s_out))


def body(slabs, lanes, populations, field_gain, front_depth, phase, solute):
    depth_here, rows_here, cols = populations.shape[1:]
    pops = populations.reshape(19, depth_here * rows_here, cols)
    vmem = pl.BlockSpec(memory_space=pltpu.VMEM)
    smem = pl.BlockSpec(memory_space=pltpu.SMEM)
    copies = 8 + 4 + 2 + (slabs - 1) + 4
    velocity, phase_next, solute_next = pl.pallas_call(
        functools.partial(kernel, slabs, lanes),
        out_shape=(
            jax.ShapeDtypeStruct((3, 128, 128), F32),
            jax.ShapeDtypeStruct(phase.shape, F32),
            jax.ShapeDtypeStruct(solute.shape, F32),
        ),
        in_specs=[vmem, vmem, smem, vmem, vmem, vmem, vmem, vmem],
        out_specs=(vmem, vmem, vmem),
        scratch_shapes=[
            pltpu.VMEM((14, 128, 128), F32),
            pltpu.VMEM((2, 128, 128), F32),
            pltpu.VMEM((2, 128, 128), F32),
            pltpu.VMEM((2, 4, 8, 128), F32),
            pltpu.VMEM((4, 8, 128), F32),
            pltpu.VMEM((2, 128, 128), F32),
            pltpu.VMEM((2, 128, 128), F32),
            pltpu.VMEM((3, 2, 16, 8, 128), F32),
            pltpu.VMEM((3, 2, 16, 8, 128), F32),
            pltpu.VMEM((slabs, 9, 8, 128), F32),
            pltpu.VMEM((slabs - 1, 9, 8, 128), F32),
            pltpu.VMEM((3, 6, 32, 256), F32),
            pltpu.VMEM((2, 2, 2, 32, 256), F32),
            pltpu.VMEM((2, 2, 2, 32, 256), F32),
            pltpu.VMEM((2, 2, 32, 128), F32),
            pltpu.VMEM((2, 2, 32, 128), F32),
            pltpu.VMEM((32, 32, 256), F32),
            pltpu.VMEM((32, 32, 256), F32),
            pltpu.SemaphoreType.DMA((copies,)),
            pltpu.SemaphoreType.DMA((copies,)),
        ],
        compiler_params=pltpu.CompilerParams(
            collective_id=0, has_side_effects=True, vmem_limit_bytes=40 * 2**20
        ),
    )(
        pops,
        field_gain.reshape(1, depth_here),
        front_depth,
        phase,
        solute,
        jnp.asarray(force_table(lanes, cols)),
        jnp.asarray(col_table()),
        jnp.asarray(row_table()),
    )
    return velocity.reshape(3, depth_here, rows_here, cols), phase_next, solute_next


def solution(mesh):
    return jax.shard_map(
        functools.partial(body, mesh.shape["gz"], mesh.shape["xy"]),
        mesh=mesh,
        in_specs=(
            P(None, "gz", "xy", None),
            P("gz"),
            P("xy", None),
            P(None, "xy", "gz"),
            P(None, "xy", "gz"),
        ),
        out_specs=(P(None, "gz", "xy", None), P(None, "xy", "gz"), P(None, "xy", "gz")),
        check_vma=False,
    )
```

profile of v0, /device:TPU:0, one launch (start us, length us, event | category | flops | bytes accessed | tf_op | source)
XLA Modules:
  0.0 54.0 jit_solution(744746109475184477)
XLA Ops:
  0.6 0.0 copy-start
  0.6 1.3 %copy-done = f32[19,32,4,128]{3,2,1,0:T(4,128)S(1)} copy-done((f32[19,32,4,128]{3,2,1,0:T(4,128)S(1)}, f32[19,32,4,128]{3,2,1,0:T(4,128)}, u32[]{:S(2)}) %copy-start) | copy-done | bytes 1245208
  1.9 0.0 copy-start.1
  1.9 1.2 %copy-done.1 = f32[32,32,256]{2,1,0:T(8,128)S(1)} copy-done((f32[32,32,256]{2,1,0:T(8,128)S(1)}, f32[32,32,256]{2,1,0:T(8,128)}, u32[]{:S(2)}) %copy-start.1) | copy-done | bytes 1048600
  3.2 0.0 copy-start.2
  3.2 1.2 %copy-done.2 = f32[32,32,256]{2,1,0:T(8,128)S(1)} copy-done((f32[32,32,256]{2,1,0:T(8,128)S(1)}, f32[32,32,256]{2,1,0:T(8,128)}, u32[]{:S(2)}) %copy-start.2) | copy-done | bytes 1048600
  4.4 0.0 copy-start.3
  4.4 0.9 %copy-done.3 = f32[128,512]{1,0:T(8,128)S(1)} copy-done((f32[128,512]{1,0:T(8,128)S(1)}, f32[128,512]{1,0:T(8,128)}, u32[]{:S(2)}) %copy-start.3) | copy-done | bytes 262168
  5.3 0.0 copy-start.4
  5.3 0.9 %copy-done.4 = f32[8,3,8,128]{3,2,1,0:T(8,128)S(1)} copy-done((f32[8,3,8,128]{3,2,1,0:T(8,128)S(1)}, f32[8,3,8,128]{3,2,1,0:T(8,128)}, u32[]{:S(2)}) %copy-start.4) | copy-done | bytes 98328
  6.2 0.0 copy-start.5
  6.2 0.7 %copy-done.5 = f32[32,8]{1,0:T(8,128)S(1)} copy-done((f32[32,8]{1,0:T(8,128)S(1)}, f32[32,8]{1,0:T(8,128)}, u32[]{:S(2)}) %copy-start.5) | copy-done | bytes 1048
  6.9 0.0 copy-start.6
  6.9 0.7 %copy-done.6 = f32[32]{0:T(128)S(1)} copy-done((f32[32]{0:T(128)S(1)}, f32[32]{0:T(128)}, u32[]{:S(2)}) %copy-start.6) | copy-done | bytes 152
  7.6 0.0 copy-start.7
  7.6 0.7 %copy-done.7 = s32[1,32]{1,0:T(1,128)S(1)} copy-done((s32[1,32]{1,0:T(1,128)S(1)}, s32[1,32]{1,0:T(1,128)}, u32[]{:S(2)}) %copy-start.7) | copy-done | bytes 152
  8.2 43.1 %shard_map.103 = (f32[3,128,128]{2,1,0:T(8,128)S(1)}, f32[32,32,256]{2,1,0:T(8,128)S(1)}, f32[32,32,256]{2,1,0:T(8,128)S(1)}) custom-call(f32[19,128,128]{2,1,0:T(8,128)S(1)} %bitcast.3, f32[1,32]{1,0:T(1,128)S(1)} %bitcast.5, s32[1,32]{1,0:T(1,128)S(1)} %copy-done.7, f32[32,32,256]{2,1,0:T(8,128)S(1)} %copy-done.1, f32[32,32,256]{2,1,0:T(8,128)S(1)} %copy-done.2, ...), custom_call_target="tpu_custom_call" | custom-call | tf_op jit(solution)/shard_map/pallas_call | solution.py:425
  51.4 0.7 %copy.14 = f32[3,32,4,128]{3,2,1,0:T(4,128)} copy(f32[3,32,4,128]{3,2,1,0:T(4,128)S(1)} %bitcast.4) | data formatting | bytes 393216
  52.0 1.0 %copy.15 = f32[32,32,256]{2,1,0:T(8,128)} copy(f32[32,32,256]{2,1,0:T(8,128)S(1)} %get-tuple-element.13) | data formatting | bytes 2097152
  53.0 1.0 %copy.16 = f32[32,32,256]{2,1,0:T(8,128)} copy(f32[32,32,256]{2,1,0:T(8,128)S(1)} %get-tuple-element.14) | data formatting | bytes 2097152
Async XLA Ops:
  0.6 1.3 %copy-start = (f32[19,32,4,128]{3,2,1,0:T(4,128)S(1)}, f32[19,32,4,128]{3,2,1,0:T(4,128)}, u32[]{:S(2)}) copy-start(f32[19,32,4,128]{3,2,1,0:T(4,128)} %param.8) | copy-start | bytes 3735556
  1.9 1.2 %copy-start.1 = (f32[32,32,256]{2,1,0:T(8,128)S(1)}, f32[32,32,256]{2,1,0:T(8,128)}, u32[]{:S(2)}) copy-start(f32[32,32,256]{2,1,0:T(8,128)} %phase.1) | copy-start | bytes 3145732
  3.2 1.2 %copy-start.2 = (f32[32,32,256]{2,1,0:T(8,128)S(1)}, f32[32,32,256]{2,1,0:T(8,128)}, u32[]{:S(2)}) copy-start(f32[32,32,256]{2,1,0:T(8,128)} %solute.1) | copy-start | bytes 3145732
  4.4 0.9 %copy-start.3 = (f32[128,512]{1,0:T(8,128)S(1)}, f32[128,512]{1,0:T(8,128)}, u32[]{:S(2)}) copy-start(f32[128,512]{1,0:T(8,128)} %constant.7.clone.ctab) | copy-start | bytes 786436
  5.3 0.9 %copy-start.4 = (f32[8,3,8,128]{3,2,1,0:T(8,128)S(1)}, f32[8,3,8,128]{3,2,1,0:T(8,128)}, u32[]{:S(2)}) copy-start(f32[8,3,8,128]{3,2,1,0:T(8,128)} %constant.6.clone.ftab) | copy-start | bytes 294916
  6.2 0.7 %copy-start.5 = (f32[32,8]{1,0:T(8,128)S(1)}, f32[32,8]{1,0:T(8,128)}, u32[]{:S(2)}) copy-start(f32[32,8]{1,0:T(8,128)} %constant.8.clone.rtab) | copy-start | bytes 3076
  6.9 0.7 %copy-start.6 = (f32[32]{0:T(128)S(1)}, f32[32]{0:T(128)}, u32[]{:S(2)}) copy-start(f32[32]{0:T(128)} %param.9) | copy-start | bytes 388
  7.6 0.7 %copy-start.7 = (s32[1,32]{1,0:T(1,128)S(1)}, s32[1,32]{1,0:T(1,128)}, u32[]{:S(2)}) copy-start(s32[1,32]{1,0:T(1,128)} %depth.1) | copy-start | bytes 388
where the time goes:
time: 54.4 us; the launch traced here: 54 us
  Pallas kernels  43.1 us (79%)
  local copies, waits for them, and re-layouts  10.2 us (19%)
  between operations  0.66 us (1%)
    pallas_call x1, Pallas kernels, body(): pl.pallas_call(functools.partial(kernel, slabs, lanes), out_shape=(jax.Sh...  43.1 us
    unnamed x19, local copies, waits for them, and re-layouts  10.2 us

commit v1 on v0

--- a/solution.py
+++ b/solution.py
@@ -76,12 +76,21 @@
 
 def kernel(
     slabs, lanes,
+    pop_hbm, gain_hbm, depth_hbm, phase_hbm, solute_hbm, ftab_hbm, ctab_hbm, rtab_hbm,
+    vel, p_low, s_low, p1, s1, fine, hx_high, hy_high,
     pop, gain, depth, phase, solute, ftab, ctab, rtab,
-    vel, p_out, s_out,
-    sums, xs, xr, zr, dr, vs, vr, v8, v8r, pk, wr, fine, ex, hx, ey, hy, p1, s1,
-    send, recv,
+    sums, xs, xr, zr, dr, vs, vr, v8, v8r, pk, wr, ex, hx, ey, hy,
+    send, recv, local,
 ):
     gz, xy = lax.axis_index("gz"), lax.axis_index("xy")
+    loads = []
+    for src, dst in (
+        (gain_hbm, gain), (ftab_hbm.at[xy], ftab), (pop_hbm, pop), (depth_hbm, depth),
+        (phase_hbm, phase), (solute_hbm, solute), (ctab_hbm, ctab), (rtab_hbm, rtab),
+    ):
+        load = pltpu.make_async_copy(src, dst, local.at[len(loads)])
+        load.start()
+        loads.append(load)
 
     def at(dz, dx):
         return (lax.rem(gz + dz + slabs, slabs), lax.rem(xy + dx + lanes, lanes))
@@ -104,10 +113,12 @@
         copy.start()
         return copy
 
+    for load in loads[:3]:
+        load.wait()
     rows32 = lax.broadcasted_iota(jnp.int32, (128, 32), 0) // 4
     cols32 = lax.broadcasted_iota(jnp.int32, (128, 32), 1)
     gain_col = jnp.sum(jnp.where(rows32 == cols32, gain[...], 0.0), axis=1, keepdims=True)
-    shape = ftab[xy]
+    shape = ftab[...]
     force = [
         jnp.broadcast_to(shape[c][None], (16, 8, 128)).reshape(128, 128) * gain_col
         for c in range(3)
@@ -207,6 +218,8 @@
         remote(sums.at[7, pl.ds(0, 8)], dr.at[3], (-1, -1)),
     ]
 
+    for load in loads[3:]:
+        load.wait()
     lane = lax.broadcasted_iota(jnp.int32, (32, 128), 1)
 
     def edges(k, carry):
@@ -224,15 +237,12 @@
     ey[0, 0] = last
     ey[0, 1] = first
 
-    def send_edges(turn):
-        return [
-            remote(ex.at[turn, 0], hx.at[turn, 0], (0, 1)),
-            remote(ex.at[turn, 1], hx.at[turn, 1], (0, -1)),
-            remote(ey.at[turn, 0], hy.at[turn, 0], (1, 0)),
-            remote(ey.at[turn, 1], hy.at[turn, 1], (-1, 0)),
-        ]
-
-    band_copies = send_edges(0)
+    band_copies = [
+        remote(ex.at[0, 0], hx.at[0, 0], (0, 1)),
+        remote(ex.at[0, 1], hx.at[0, 1], (0, -1)),
+        remote(ey.at[0, 0], hy.at[0, 0], (1, 0)),
+        remote(ey.at[0, 1], hy.at[0, 1], (-1, 0)),
+    ]
     for copy in flow_copies:
         copy.wait()
 
@@ -305,29 +315,34 @@
     lane8 = lax.broadcasted_iota(jnp.int32, (8, 128), 1)
     tile_of = lane8 // 4
     group_of = lane8 // 32
-    total_z = 32 * slabs
+    tiles_z = 8 * slabs
     none8 = jnp.zeros((8, 128), F32)
+
+    def gather(tile, carry):
+        here_z = depth[0, tile]
+        prev_z = jnp.where(here_z == 0, tiles_z - 1, here_z - 1)
+        next_z = jnp.where(here_z == tiles_z - 1, 0, here_z + 1)
+        masks, places = [], []
+        for at_tile in (prev_z, here_z, next_z):
+            masks.append(tile_of == jnp.where((at_tile >> 3) == gz, tile, -1))
+            places.append((at_tile & 7) * 2)
+        picks = [(0, 1, places[0] + 1)]
+        picks += [(1, i % 2, places[1] + i // 2) for i in range(4)]
+        picks += [(2, 0, places[2])]
+        out = []
+        for c in range(3):
+            for dz, (m, par, half) in enumerate(picks):
+                out.append(jnp.where(masks[m], v8[c, par, half], carry[12 * c + 2 * dz]))
+                out.append(jnp.where(masks[m], v8r[c, par, half], carry[12 * c + 2 * dz + 1]))
+        return tuple(out)
+
+    items = lax.fori_loop(0, 8 * slabs, gather, (none8,) * 36)
     for c in range(3):
-
-        def gather(tile, carry):
-            carry = list(carry)
-            start = depth[0, tile] * 4 - 1 + total_z
-            for dz in range(6):
-                z = lax.rem(start + dz, total_z)
-                z_here = lax.rem(z, 32)
-                mark = jnp.where(z // 32 == gz, tile, -1)
-                here = tile_of == mark
-                par, half = lax.rem(z_here, 2), z_here // 2
-                carry[2 * dz] = jnp.where(here, v8[c, par, half], carry[2 * dz])
-                carry[2 * dz + 1] = jnp.where(here, v8r[c, par, half], carry[2 * dz + 1])
-            return tuple(carry)
-
-        items = lax.fori_loop(0, 8 * slabs, gather, (none8,) * 12)
         for target in range(slabs):
             for m in range(3):
                 out = none8
                 for g in range(4):
-                    item = items[4 * m + g]
+                    item = items[12 * c + 4 * m + g]
                     s = (32 * (g - target)) % 128
                     moved = item if s == 0 else pltpu.roll(item, s, 1)
                     out = jnp.where(group_of == g, moved, out)
@@ -353,85 +368,169 @@
                 precision=lax.Precision.HIGHEST, preferred_element_type=F32,
             )
 
-    big_row = lax.broadcasted_iota(jnp.int32, (32, 256), 0)
-    big_lane = lax.broadcasted_iota(jnp.int32, (32, 256), 1)
-
-    def band(turn, src, dst):
-        def plane(k, carry):
-            before, after, first, last = carry
-            low = (2 * k + 9) // 16
-            frac = lax.rem(2 * k + 9, 16).astype(F32) * (1.0 / 16.0)
-            flow = []
-            for c in range(3):
-                lower = fine[c, low]
-                flow.append(lower + frac * (fine[c, low + 1] - lower))
-            above, below = jnp.minimum(k + 1, 31), jnp.maximum(k - 1, 0)
-            results = []
-            for n, ref in enumerate(src):
-                mid = ref[k]
-                zu, zd = ref[above], ref[below]
-                xu = jnp.where(
-                    big_row == 31, hx[turn, 1, n, pl.ds(k, 1), :], pltpu.roll(mid, 31, 0)
-                )
-                xd = jnp.where(
-                    big_row == 0, hx[turn, 0, n, pl.ds(k, 1), :], pltpu.roll(mid, 1, 0)
-                )
-                yu = jnp.where(
-                    big_lane == 255, after[:, 32 * n:32 * n + 1], pltpu.roll(mid, 255, 1)
-                )
-                yd = jnp.where(
-                    big_lane == 0, before[:, 32 * n:32 * n + 1], pltpu.roll(mid, 1, 1)
-                )
-                drift = flow[0] * (zu - zd) + flow[1] * (xu - xd) + flow[2] * (yu - yd)
-                zz = zu + zd
-                side = (xu + xd) + (yu + yd)
-                results.append((mid, zz, side, drift))
-            p, zz, side, drift = results[0]
-            s = results[1][0]
-            drive = p * (1.0 - p) * (0.4 * p + 0.2 * s - 0.4)
-            change = 0.15 * zz + 0.1 * side - 0.7 * p - drift + drive
-            p_new = p + change
-            s, zz, side, drift = results[1]
-            s_new = 0.4 * s + 0.1 * (zz + side) - drift + 0.85 * s * change
-            dst[0][k] = p_new
-            dst[1][k] = s_new
-            if turn == 0:
-                for n, new in enumerate((p_new, s_new)):
-                    ex[1, 0, n, pl.ds(k, 1), :] = new[31:32, :]
-                    ex[1, 1, n, pl.ds(k, 1), :] = new[0:1, :]
-                    here = lane == k + 32 * n
-                    last = jnp.where(here, new[:, 255:256], last)
-                    first = jnp.where(here, new[:, 0:1], first)
-            return pltpu.roll(before, 127, 1), pltpu.roll(after, 127, 1), first, last
-
-        return lax.fori_loop(0, 32, plane, (hy[turn, 0], hy[turn, 1], nothing, nothing))
+    def keep_edges(k, results, carry):
+        last, first = carry
+        for n, (left, right) in enumerate(results):
+            ex[1, 0, n, pl.ds(k, 1), :] = jnp.concatenate([left[31:32], right[31:32]], axis=1)
+            ex[1, 1, n, pl.ds(k, 1), :] = jnp.concatenate([left[0:1], right[0:1]], axis=1)
+            here = lane == k + 32 * n
+            last = jnp.where(here, right[:, 127:128], last)
+            first = jnp.where(here, left[:, 0:1], first)
+        return last, first
 
     for copy in band_copies:
         copy.wait()
-    _, _, first, last = band(0, (phase, solute), (p1, s1))
-    ey[1, 0] = last
-    ey[1, 1] = first
-    for copy in send_edges(1):
-        copy.wait()
-    band(1, (p1, s1), (p_out, s_out))
+    sides = (hy[0, 0], hy[0, 1])
+    halves = []
+    for half in range(2):
+        ks = slice(16 * half, 16 * half + 16)
+
+        def first_step(k, carry):
+            results = plane(k, (phase, solute), fine, hx.at[0], k, carry[:2])
+            for dst, (left, right) in zip((p1, s1), results):
+                dst[k, :, :128] = left
+                dst[k, :, 128:] = right
+            return next_sides(carry[:2]) + keep_edges(k, results, carry[2:])
+
+        *sides, last, first = lax.fori_loop(
+            16 * half, 16 * half + 16, first_step, (*sides, nothing, nothing)
+        )
+        ey[1 + half, 0] = last
+        ey[1 + half, 1] = first
+        halves.append([
+            remote(ex.at[1, 0, :, ks], hx.at[1, 0, :, ks], (0, 1)),
+            remote(ex.at[1, 1, :, ks], hx.at[1, 1, :, ks], (0, -1)),
+            remote(ey.at[1 + half, 0], hy.at[1 + half, 0], (1, 0)),
+            remote(ey.at[1 + half, 1], hy.at[1 + half, 1], (-1, 0)),
+        ])
+    for copy in halves[0]:
+        copy.wait()
+
+    def second_step(k, carry):
+        results = plane(k, (p1, s1), fine, hx.at[1], k, carry)
+        for dst, (left, right) in zip((p_low, s_low), results):
+            dst[k, :, :128] = left
+            dst[k, :, 128:] = right
+        return next_sides(carry)
+
+    lax.fori_loop(0, 16, second_step, (hy[1, 0], hy[1, 1]))
+    for copy in halves[1]:
+        copy.wait()
+    hx_high[...] = hx[1, :, :, 16:32]
+    hy_high[...] = hy[2]
+
+
+def next_sides(sides):
+    return tuple(pltpu.roll(v, 127, 1) for v in sides)
+
+
+def plane(k, src, fine, rows, row_at, sides):
+    sub = lax.broadcasted_iota(jnp.int32, (32, 128), 0)
+    lane = lax.broadcasted_iota(jnp.int32, (32, 128), 1)
+    before, after = sides
+    low = (2 * k + 9) >> 4
+    frac = ((2 * k + 9) & 15).astype(F32) * (1.0 / 16.0)
+    above, below = jnp.minimum(k + 1, 31), jnp.maximum(k - 1, 0)
+    along_y = []
+    for n, ref in enumerate(src):
+        left, right = ref[k, :, :128], ref[k, :, 128:]
+        left_up, right_up = pltpu.roll(left, 127, 1), pltpu.roll(right, 127, 1)
+        left_dn, right_dn = pltpu.roll(left, 1, 1), pltpu.roll(right, 1, 1)
+        edge_up, edge_dn = after[:, 32 * n:32 * n + 1], before[:, 32 * n:32 * n + 1]
+        along_y.append((
+            (jnp.where(lane == 127, right_up, left_up), jnp.where(lane == 0, edge_dn, left_dn)),
+            (jnp.where(lane == 127, edge_up, right_up), jnp.where(lane == 0, left_dn, right_dn)),
+        ))
+    out_p, out_s = [], []
+    for half in range(2):
+        cols = slice(128 * half, 128 * half + 128)
+        flow = []
+        for c in range(3):
+            lower = fine[c, low, :, cols]
+            flow.append(lower + frac * (fine[c, low + 1, :, cols] - lower))
+        terms = []
+        for n, ref in enumerate(src):
+            mid = ref[k, :, cols]
+            zu, zd = ref[above, :, cols], ref[below, :, cols]
+            row_up = rows[1, n, pl.ds(row_at, 1), :][:, cols]
+            row_dn = rows[0, n, pl.ds(row_at, 1), :][:, cols]
+            xu = jnp.where(sub == 31, row_up, pltpu.roll(mid, 31, 0))
+            xd = jnp.where(sub == 0, row_dn, pltpu.roll(mid, 1, 0))
+            yu, yd = along_y[n][half]
+            drift = flow[0] * (zu - zd) + flow[1] * (xu - xd) + flow[2] * (yu - yd)
+            terms.append((mid, zu + zd, (xu + xd) + (yu + yd), drift))
+        p, zz, side, drift = terms[0]
+        s, zz_s, side_s, drift_s = terms[1]
+        drive = p * (1.0 - p) * (0.4 * p + 0.2 * s - 0.4)
+        change = 0.15 * zz + 0.1 * side - 0.7 * p - drift + drive
+        out_p.append(p + change)
+        out_s.append(0.4 * s + 0.1 * (zz_s + side_s) - drift_s + 0.85 * s * change)
+    return out_p, out_s
+
+
+def finish(
+    vel, p_low, s_low, p1, s1, fine, hx_high, hy_high,
+    vel_out, p_out, s_out, p_high, s_high, sems,
+):
+    copies = [
+        pltpu.make_async_copy(vel, vel_out, sems.at[0]),
+        pltpu.make_async_copy(p_low, p_out.at[0:16], sems.at[1]),
+        pltpu.make_async_copy(s_low, s_out.at[0:16], sems.at[2]),
+    ]
+    for copy in copies:
+        copy.start()
+    sides = tuple(pltpu.roll(hy_high[i], 112, 1) for i in range(2))
+    for part in range(2):
+
+        def step(k, carry):
+            results = plane(k + 16, (p1, s1), fine, hx_high, k, carry)
+            for dst, (left, right) in zip((p_high, s_high), results):
+                dst[k, :, :128] = left
+                dst[k, :, 128:] = right
+            return next_sides(carry)
+
+        sides = lax.fori_loop(8 * part, 8 * part + 8, step, sides)
+        here = slice(8 * part, 8 * part + 8)
+        there = slice(16 + 8 * part, 24 + 8 * part)
+        for n, (src, dst) in enumerate(((p_high, p_out), (s_high, s_out))):
+            copy = pltpu.make_async_copy(
+                src.at[here], dst.at[there], sems.at[3 + 2 * part + n]
+            )
+            copy.start()
+            copies.append(copy)
+    for copy in copies:
+        copy.wait()
 
 
 def body(slabs, lanes, populations, field_gain, front_depth, phase, solute):
     depth_here, rows_here, cols = populations.shape[1:]
     pops = populations.reshape(19, depth_here * rows_here, cols)
     vmem = pl.BlockSpec(memory_space=pltpu.VMEM)
-    smem = pl.BlockSpec(memory_space=pltpu.SMEM)
-    copies = 8 + 4 + 2 + (slabs - 1) + 4
-    velocity, phase_next, solute_next = pl.pallas_call(
+    anywhere = pl.BlockSpec(memory_space=pltpu.HBM)
+    copies = 8 + 4 + 2 + (slabs - 1) + 8
+    passed = pl.pallas_call(
         functools.partial(kernel, slabs, lanes),
         out_shape=(
             jax.ShapeDtypeStruct((3, 128, 128), F32),
+            jax.ShapeDtypeStruct((16, 32, 256), F32),
+            jax.ShapeDtypeStruct((16, 32, 256), F32),
             jax.ShapeDtypeStruct(phase.shape, F32),
             jax.ShapeDtypeStruct(solute.shape, F32),
+            jax.ShapeDtypeStruct((3, 6, 32, 256), F32),
+            jax.ShapeDtypeStruct((2, 2, 16, 256), F32),
+            jax.ShapeDtypeStruct((2, 32, 128), F32),
         ),
-        in_specs=[vmem, vmem, smem, vmem, vmem, vmem, vmem, vmem],
-        out_specs=(vmem, vmem, vmem),
+        in_specs=[anywhere] * 8,
+        out_specs=(vmem,) * 8,
         scratch_shapes=[
+            pltpu.VMEM(pops.shape, F32),
+            pltpu.VMEM((1, depth_here), F32),
+            pltpu.SMEM(front_depth.shape, jnp.int32),
+            pltpu.VMEM(phase.shape, F32),
+            pltpu.VMEM(solute.shape, F32),
+            pltpu.VMEM((3, 8, cols), F32),
+            pltpu.VMEM((128, 512), F32),
+            pltpu.VMEM((32, 8), F32),
             pltpu.VMEM((14, 128, 128), F32),
             pltpu.VMEM((2, 128, 128), F32),
             pltpu.VMEM((2, 128, 128), F32),
@@ -443,18 +542,16 @@
             pltpu.VMEM((3, 2, 16, 8, 128), F32),
             pltpu.VMEM((slabs, 9, 8, 128), F32),
             pltpu.VMEM((slabs - 1, 9, 8, 128), F32),
-            pltpu.VMEM((3, 6, 32, 256), F32),
             pltpu.VMEM((2, 2, 2, 32, 256), F32),
             pltpu.VMEM((2, 2, 2, 32, 256), F32),
-            pltpu.VMEM((2, 2, 32, 128), F32),
-            pltpu.VMEM((2, 2, 32, 128), F32),
-            pltpu.VMEM((32, 32, 256), F32),
-            pltpu.VMEM((32, 32, 256), F32),
+            pltpu.VMEM((3, 2, 32, 128), F32),
+            pltpu.VMEM((3, 2, 32, 128), F32),
             pltpu.SemaphoreType.DMA((copies,)),
             pltpu.SemaphoreType.DMA((copies,)),
+            pltpu.SemaphoreType.DMA((8,)),
         ],
         compiler_params=pltpu.CompilerParams(
-            collective_id=0, has_side_effects=True, vmem_limit_bytes=40 * 2**20
+            collective_id=0, has_side_effects=True, vmem_limit_bytes=24 * 2**20
         ),
     )(
         pops,
@@ -466,6 +563,22 @@
         jnp.asarray(col_table()),
         jnp.asarray(row_table()),
     )
+    velocity, phase_next, solute_next = pl.pallas_call(
+        finish,
+        out_shape=(
+            jax.ShapeDtypeStruct((3, 128, 128), F32),
+            jax.ShapeDtypeStruct(phase.shape, F32),
+            jax.ShapeDtypeStruct(solute.shape, F32),
+        ),
+        in_specs=[vmem] * 8,
+        out_specs=(anywhere,) * 3,
+        scratch_shapes=[
+            pltpu.VMEM((16, 32, 256), F32),
+            pltpu.VMEM((16, 32, 256), F32),
+            pltpu.SemaphoreType.DMA((7,)),
+        ],
+        compiler_params=pltpu.CompilerParams(vmem_limit_bytes=16 * 2**20),
+    )(*passed)
     return velocity.reshape(3, depth_here, rows_here, cols), phase_next, solute_next
 
 

time: 54.4 us -> 43.3 us (0.80)
  Pallas kernels: 43.1 us -> 34.7 us
  local copies, waits for them, and re-layouts: 10.2 us -> 7.6 us
    pallas_call x1, Pallas kernels: 43.1 us -> 31.6 us  [body(): pl.pallas_call(functools.partial(kernel, slabs, lanes), out_shape=(jax.Sh...]
    pallas_call x0 -> x1, Pallas kernels: none -> 3.09 us  [body(): pl.pallas_call(finish, out_shape=(jax.ShapeDtypeStruct((3, 128, 128), F32...]
    unnamed x19 -> x16, local copies, waits for them, and re-layouts: 10.2 us -> 7.6 us
where the time goes in v1:
time: 43.3 us; the launch traced here: 42.9 us
  Pallas kernels  34.7 us (80%)
  local copies, waits for them, and re-layouts  7.6 us (18%)
  between operations  0.66 us (2%)
    pallas_call x1, Pallas kernels, body(): pl.pallas_call(functools.partial(kernel, slabs, lanes), out_shape=(jax.Sh...  31.6 us
    unnamed x16, local copies, waits for them, and re-layouts  7.6 us
    pallas_call x1, Pallas kernels, body(): pl.pallas_call(finish, out_shape=(jax.ShapeDtypeStruct((3, 128, 128), F32...  3.09 us

profile of v1, /device:TPU:0, one launch (start us, length us, event | category | flops | bytes accessed | tf_op | source)
XLA Modules:
  0.0 42.9 jit_solution(5815514436729223687)
XLA Ops:
  0.6 0.0 copy-start
  0.6 1.3 %copy-done = f32[19,32,4,128]{3,2,1,0:T(4,128)S(1)} copy-done((f32[19,32,4,128]{3,2,1,0:T(4,128)S(1)}, f32[19,32,4,128]{3,2,1,0:T(4,128)}, u32[]{:S(2)}) %copy-start) | copy-done | bytes 1245208
  1.9 0.0 copy-start.1
  1.9 1.2 %copy-done.1 = f32[32,32,256]{2,1,0:T(8,128)S(1)} copy-done((f32[32,32,256]{2,1,0:T(8,128)S(1)}, f32[32,32,256]{2,1,0:T(8,128)}, u32[]{:S(2)}) %copy-start.1) | copy-done | bytes 1048600
  3.2 0.0 copy-start.2
  3.2 1.2 %copy-done.2 = f32[32,32,256]{2,1,0:T(8,128)S(1)} copy-done((f32[32,32,256]{2,1,0:T(8,128)S(1)}, f32[32,32,256]{2,1,0:T(8,128)}, u32[]{:S(2)}) %copy-start.2) | copy-done | bytes 1048600
  4.4 0.0 copy-start.3
  4.4 0.9 %copy-done.3 = f32[128,512]{1,0:T(8,128)S(1)} copy-done((f32[128,512]{1,0:T(8,128)S(1)}, f32[128,512]{1,0:T(8,128)}, u32[]{:S(2)}) %copy-start.3) | copy-done | bytes 262168
  5.3 0.0 copy-start.4
  5.3 0.9 %copy-done.4 = f32[8,3,8,128]{3,2,1,0:T(8,128)S(1)} copy-done((f32[8,3,8,128]{3,2,1,0:T(8,128)S(1)}, f32[8,3,8,128]{3,2,1,0:T(8,128)}, u32[]{:S(2)}) %copy-start.4) | copy-done | bytes 98328
  6.2 0.0 copy-start.5
  6.2 0.7 %copy-done.5 = f32[32,8]{1,0:T(8,128)S(1)} copy-done((f32[32,8]{1,0:T(8,128)S(1)}, f32[32,8]{1,0:T(8,128)}, u32[]{:S(2)}) %copy-start.5) | copy-done | bytes 1048
  6.9 0.0 copy-start.6
  6.9 0.7 %copy-done.6 = f32[32]{0:T(128)S(1)} copy-done((f32[32]{0:T(128)S(1)}, f32[32]{0:T(128)}, u32[]{:S(2)}) %copy-start.6) | copy-done | bytes 152
  7.6 0.0 copy-start.7
  7.6 0.7 %copy-done.7 = s32[1,32]{1,0:T(1,128)S(1)} copy-done((s32[1,32]{1,0:T(1,128)S(1)}, s32[1,32]{1,0:T(1,128)}, u32[]{:S(2)}) %copy-start.7) | copy-done | bytes 152
  8.2 31.6 %shard_map.103 = (f32[3,128,128]{2,1,0:T(8,128)S(1)}, f32[16,32,256]{2,1,0:T(8,128)S(1)}, f32[16,32,256]{2,1,0:T(8,128)S(1)}, f32[32,32,256]{2,1,0:T(8,128)S(1)}...) custom-call(f32[19,128,128]{2,1,0:T(8,128)S(1)} %bitcast.3, ...), custom_call_target="tpu_custom_call" | custom-call | tf_op jit(solution)/shard_map/pallas_call | solution.py:511
  39.8 3.1 %shard_map.104 = (f32[3,128,128]{2,1,0:T(8,128)}, f32[32,32,256]{2,1,0:T(8,128)}, f32[32,32,256]{2,1,0:T(8,128)}) custom-call(f32[3,128,128]{2,1,0:T(8,128)S(1)} %get-tuple-element.14.vel, f32[16,32,256]{2,1,0:T(8,128)S(1)} %get-tuple-element.15.p_low, f32[16,32,256]{2,1,0:T(8,128)S(1)} %get-tuple-element.16.s_low, f32[32,32,256]{2,1,0:T(8,128)S(1)} %get-tuple-element.17.p1, ...), custom_call_target="tpu_custom_call" | custom-call | tf_op jit(solution)/shard_map/pallas_call | solution.py:566
Async XLA Ops:
  0.6 1.3 %copy-start = (f32[19,32,4,128]{3,2,1,0:T(4,128)S(1)}, f32[19,32,4,128]{3,2,1,0:T(4,128)}, u32[]{:S(2)}) copy-start(f32[19,32,4,128]{3,2,1,0:T(4,128)} %param.8) | copy-start | bytes 3735556
  1.9 1.2 %copy-start.1 = (f32[32,32,256]{2,1,0:T(8,128)S(1)}, f32[32,32,256]{2,1,0:T(8,128)}, u32[]{:S(2)}) copy-start(f32[32,32,256]{2,1,0:T(8,128)} %phase_hbm.1) | copy-start | bytes 3145732
  3.2 1.2 %copy-start.2 = (f32[32,32,256]{2,1,0:T(8,128)S(1)}, f32[32,32,256]{2,1,0:T(8,128)}, u32[]{:S(2)}) copy-start(f32[32,32,256]{2,1,0:T(8,128)} %solute_hbm.1) | copy-start | bytes 3145732
  4.4 0.9 %copy-start.3 = (f32[128,512]{1,0:T(8,128)S(1)}, f32[128,512]{1,0:T(8,128)}, u32[]{:S(2)}) copy-start(f32[128,512]{1,0:T(8,128)} %constant.7.clone.ctab_hbm) | copy-start | bytes 786436
  5.3 0.9 %copy-start.4 = (f32[8,3,8,128]{3,2,1,0:T(8,128)S(1)}, f32[8,3,8,128]{3,2,1,0:T(8,128)}, u32[]{:S(2)}) copy-start(f32[8,3,8,128]{3,2,1,0:T(8,128)} %constant.6.clone.ftab_hbm) | copy-start | bytes 294916
  6.2 0.7 %copy-start.5 = (f32[32,8]{1,0:T(8,128)S(1)}, f32[32,8]{1,0:T(8,128)}, u32[]{:S(2)}) copy-start(f32[32,8]{1,0:T(8,128)} %constant.8.clone.rtab_hbm) | copy-start | bytes 3076
  6.9 0.7 %copy-start.6 = (f32[32]{0:T(128)S(1)}, f32[32]{0:T(128)}, u32[]{:S(2)}) copy-start(f32[32]{0:T(128)} %param.9) | copy-start | bytes 388
  7.6 0.7 %copy-start.7 = (s32[1,32]{1,0:T(1,128)S(1)}, s32[1,32]{1,0:T(1,128)}, u32[]{:S(2)}) copy-start(s32[1,32]{1,0:T(1,128)} %depth_hbm.1) | copy-start | bytes 388

commit v2 on v1

--- a/solution.py
+++ b/solution.py
@@ -554,14 +554,14 @@
             collective_id=0, has_side_effects=True, vmem_limit_bytes=24 * 2**20
         ),
     )(
-        pops,
+        *(pltpu.with_memory_space_constraint(x, pltpu.HBM) for x in (pops,
         field_gain.reshape(1, depth_here),
         front_depth,
         phase,
         solute,
         jnp.asarray(force_table(lanes, cols)),
         jnp.asarray(col_table()),
-        jnp.asarray(row_table()),
+        jnp.asarray(row_table())))
     )
     velocity, phase_next, solute_next = pl.pallas_call(
         finish,

time: 43.3 us -> 35.4 us (0.82)
  local copies, waits for them, and re-layouts: 7.6 us -> 0 us
    unnamed x16 -> x0, local copies, waits for them, and re-layouts: 7.6 us -> none
where the time goes in v2:
time: 35.4 us; the launch traced here: 35.2 us
  Pallas kernels  34.6 us (98%)
  between operations  0.64 us (2%)
    pallas_call x1, Pallas kernels, body(): pl.pallas_call(functools.partial(kernel, slabs, lanes), out_shape=(jax.Sh...  31.5 us
    pallas_call x1, Pallas kernels, body(): pl.pallas_call(finish, out_shape=(jax.ShapeDtypeStruct((3, 128, 128), F32...  3.08 us

profile of v2, /device:TPU:0, one launch (start us, length us, event | category | flops | bytes accessed | tf_op | source)
XLA Modules:
  0.0 35.2 jit_solution(5695790987571358799)
XLA Ops:
  0.6 31.5 %shard_map.103 = (f32[3,128,128]{2,1,0:T(8,128)S(1)}, f32[16,32,256]{2,1,0:T(8,128)S(1)}, f32[16,32,256]{2,1,0:T(8,128)S(1)}, f32[32,32,256]{2,1,0:T(8,128)S(1)}...) custom-call(f32[19,128,128]{2,1,0:T(8,128)} %bitcast.3, ...), custom_call_target="tpu_custom_call" | custom-call | tf_op jit(solution)/shard_map/pallas_call | solution.py:511
  32.2 3.1 %shard_map.104 = (f32[3,128,128]{2,1,0:T(8,128)}, f32[32,32,256]{2,1,0:T(8,128)}, f32[32,32,256]{2,1,0:T(8,128)}) custom-call(f32[3,128,128]{2,1,0:T(8,128)S(1)} %get-tuple-element.14.vel, f32[16,32,256]{2,1,0:T(8,128)S(1)} %get-tuple-element.15.p_low, f32[16,32,256]{2,1,0:T(8,128)S(1)} %get-tuple-element.16.s_low, f32[32,32,256]{2,1,0:T(8,128)S(1)} %get-tuple-element.17.p1, ...), custom_call_target="tpu_custom_call" | custom-call | tf_op jit(solution)/shard_map/pallas_call | solution.py:566

commit v3 on v2

--- a/solution.py
+++ b/solution.py
@@ -187,7 +187,7 @@
         put(12, 0, 5, 6)
         return carry
 
-    lax.fori_loop(0, 16, collide, 0)
+    lax.fori_loop(0, 16, collide, 0, unroll=2)
 
     row = lax.broadcasted_iota(jnp.int32, (128, 128), 0)
     x_of = lax.rem(row, 4)
@@ -233,7 +233,7 @@
         return first, last
 
     nothing = jnp.zeros((32, 128), F32)
-    first, last = lax.fori_loop(0, 32, edges, (nothing, nothing))
+    first, last = lax.fori_loop(0, 32, edges, (nothing, nothing), unroll=4)
     ey[0, 0] = last
     ey[0, 1] = first
 
@@ -336,7 +336,7 @@
                 out.append(jnp.where(masks[m], v8r[c, par, half], carry[12 * c + 2 * dz + 1]))
         return tuple(out)
 
-    items = lax.fori_loop(0, 8 * slabs, gather, (none8,) * 36)
+    items = lax.fori_loop(0, 8 * slabs, gather, (none8,) * 36, unroll=4)
     for c in range(3):
         for target in range(slabs):
             for m in range(3):
@@ -393,7 +393,7 @@
             return next_sides(carry[:2]) + keep_edges(k, results, carry[2:])
 
         *sides, last, first = lax.fori_loop(
-            16 * half, 16 * half + 16, first_step, (*sides, nothing, nothing)
+            16 * half, 16 * half + 16, first_step, (*sides, nothing, nothing), unroll=2
         )
         ey[1 + half, 0] = last
         ey[1 + half, 1] = first
@@ -413,7 +413,7 @@
             dst[k, :, 128:] = right
         return next_sides(carry)
 
-    lax.fori_loop(0, 16, second_step, (hy[1, 0], hy[1, 1]))
+    lax.fori_loop(0, 16, second_step, (hy[1, 0], hy[1, 1]), unroll=2)
     for copy in halves[1]:
         copy.wait()
     hx_high[...] = hx[1, :, :, 16:32]
@@ -489,7 +489,7 @@
                 dst[k, :, 128:] = right
             return next_sides(carry)
 
-        sides = lax.fori_loop(8 * part, 8 * part + 8, step, sides)
+        sides = lax.fori_loop(8 * part, 8 * part + 8, step, sides, unroll=2)
         here = slice(8 * part, 8 * part + 8)
         there = slice(16 + 8 * part, 24 + 8 * part)
         for n, (src, dst) in enumerate(((p_high, p_out), (s_high, s_out))):

time: 35.4 us -> 33.9 us (0.958)
  Pallas kernels: 34.6 us -> 33.1 us
    pallas_call x1, Pallas kernels: 31.5 us -> 30.2 us  [body(): pl.pallas_call(functools.partial(kernel, slabs, lanes), out_shape=(jax.Sh...]
where the time goes in v3:
time: 33.9 us; the launch traced here: 33.7 us
  Pallas kernels  33.1 us (98%)
  between operations  0.64 us (2%)
    pallas_call x1, Pallas kernels, body(): pl.pallas_call(functools.partial(kernel, slabs, lanes), out_shape=(jax.Sh...  30.2 us
    pallas_call x1, Pallas kernels, body(): pl.pallas_call(finish, out_shape=(jax.ShapeDtypeStruct((3, 128, 128), F32...  2.88 us

profile of v3, /device:TPU:0, one launch (start us, length us, event | category | flops | bytes accessed | tf_op | source)
XLA Modules:
  0.0 33.7 jit_solution(13120610975958932292)
XLA Ops:
  0.6 30.2 %shard_map.103 = (f32[3,128,128]{2,1,0:T(8,128)S(1)}, f32[16,32,256]{2,1,0:T(8,128)S(1)}, f32[16,32,256]{2,1,0:T(8,128)S(1)}, f32[32,32,256]{2,1,0:T(8,128)S(1)}...) custom-call(f32[19,128,128]{2,1,0:T(8,128)} %bitcast.3, ...), custom_call_target="tpu_custom_call" | custom-call | tf_op jit(solution)/shard_map/pallas_call | solution.py:511
  30.8 2.9 %shard_map.104 = (f32[3,128,128]{2,1,0:T(8,128)}, f32[32,32,256]{2,1,0:T(8,128)}, f32[32,32,256]{2,1,0:T(8,128)}) custom-call(f32[3,128,128]{2,1,0:T(8,128)S(1)} %get-tuple-element.14.vel, f32[16,32,256]{2,1,0:T(8,128)S(1)} %get-tuple-element.15.p_low, f32[16,32,256]{2,1,0:T(8,128)S(1)} %get-tuple-element.16.s_low, f32[32,32,256]{2,1,0:T(8,128)S(1)} %get-tuple-element.17.p1, ...), custom_call_target="tpu_custom_call" | custom-call | tf_op jit(solution)/shard_map/pallas_call | solution.py:566
